TPU v7x, 256 devices: a whole 4x4x8 slice. The times are simulated.
256 devices in a mesh: dp: 2 (over x_lo), seq: 16 (over z, core), fsdp: 8 (over x_hi, y).
Axes of the slice: x: 4 (x_hi: 2, x_lo: 2; x = x_hi * 2 + x_lo), y: 4, z: 8, core: 2. Of those that a mesh axis runs over, the one named last changes fastest.
Arguments:
- queries_raw: bfloat16 [16, 4096, 2048], P(('dp', 'fsdp'), 'seq'), parts along dimension 0, may hold values from -6 to 6
- keys_values: bfloat16 [16, 4096, 2048], P(('dp', 'fsdp'), 'seq'), parts along dimension 0, may hold values from -6 to 6
- doc_ids: int32 [16, 4096], P(('dp', 'fsdp')), parts along dimension 0, may hold values from 0 to 3, never falling along the last dimension, each value on 1 to 2048 neighbouring positions
- q_gain: float32 [128], replicated, may hold values from 0.6 to 7
- k_gain: float32 [128], replicated, may hold values from 0.6 to 7
- out_weight: bfloat16 [2048, 5376], P('fsdp'), may hold values from -0.125 to 0.125
- post_gain: float32 [5376], replicated, may hold values from 0.25 to 1.75
Outputs:
- layer_out: bfloat16 [16, 4096, 5376], P(('dp', 'fsdp'), 'seq'), parts along dimension 0
There are 2 independent parts, one for each index of `dp`. A program takes and returns all parts, laid end to end along the dimension named above; an argument that names none is the same for every part. Nothing has to cross between parts.
Inputs may be any that keep to these rules, and one draw needn't show every extreme that they name: `doc_ids`: each slab's document numbers never fall; a document has at most 2048 tokens, and one has exactly that many.
All inputs are finite; a program needn't handle non-finite values.
Results may differ from a plain program's by a relative error of at most 0.008.
The roundings to bfloat16 on the way count: a program that leaves them out, or rounds other values in their place, can miss the bound.
Values may be sent and summed in bfloat16 or wider, within the bound.
No kernel may reach another device: no remote copies, remote signals or barrier semaphores. Data moves between devices by JAX's collectives and lax.ppermute only.
A program may use at most 128 MiB of HBM per device.

v0:
```python
import math
import jax
import jax.numpy as jnp
from jax import lax
from jax.sharding import PartitionSpec as P

WINDOW = 1024
attn_scale = 168.0 ** (-0.5)
norm_eps = 1e-06


def from_behind(block, axis, distance):
    devices = range(lax.axis_size(axis))
    route = [(i - distance, i) for i in devices if i - distance in devices]
    return lax.ppermute(block, axis, route)


def doc_positions(ids):
    count = ids.shape[0]
    index = jnp.arange(count, dtype=jnp.int32)
    flags = jnp.concatenate([jnp.ones((1,), bool), ids[1:] != ids[:-1]])
    starts = lax.cummax(jnp.where(flags, index, 0), axis=0)
    return index - starts


def norm_rope(inputs, gain, positions):
    values = inputs.astype(jnp.float32)
    meansq = jnp.mean(values * values, axis=-1, keepdims=True)
    scaled = values * lax.rsqrt(meansq + norm_eps) * gain
    width = values.shape[-1]
    half = width // 2
    inverse = 10000.0 ** (-(jnp.arange(half, dtype=jnp.float32) * 2.0 / width))
    angles = positions.astype(jnp.float32)[:, None] * inverse[None, :]
    cosine = jnp.cos(angles)[:, None, :]
    sine = jnp.sin(angles)[:, None, :]
    first = scaled[..., :half]
    second = scaled[..., half:]
    rotated = jnp.concatenate(
        [first * cosine - second * sine, second * cosine + first * sine], axis=-1
    )
    return rotated.astype(jnp.bfloat16)


def on_device(queries_raw, keys_values, doc_ids, q_gain, k_gain, out_weight, post_gain):
    tokens = queries_raw.shape[1]
    head_dim = q_gain.shape[0]
    features = queries_raw.shape[2]
    heads = features // head_dim
    kv_cols = keys_values.shape[2] // 2
    kv_heads = kv_cols // head_dim
    group = heads // kv_heads
    seq_index = lax.axis_index("seq")
    begin = seq_index * tokens
    ids_all = doc_ids[0]
    positions = lax.dynamic_slice_in_dim(doc_positions(ids_all), begin, tokens, 0)
    queries = norm_rope(queries_raw[0].reshape(tokens, heads, head_dim), q_gain, positions)
    queries = queries.reshape(tokens, kv_heads, group, head_dim)
    raw_pairs = keys_values[0]
    keys = norm_rope(raw_pairs[:, :kv_cols].reshape(tokens, kv_heads, head_dim), k_gain, positions)
    local = jnp.concatenate([keys.reshape(tokens, kv_cols), raw_pairs[:, kv_cols:]], axis=1)
    reach = (WINDOW - 2) // tokens + 1
    pieces = []
    for offset in range(reach, 0, -1):
        pieces.append(from_behind(local, "seq", offset))
    pieces.append(local)
    joined = jnp.concatenate(pieces, axis=0)
    span = (reach + 1) * tokens
    ids_pad = jnp.concatenate([jnp.full((reach * tokens,), -1, jnp.int32), ids_all])
    key_ids = lax.dynamic_slice_in_dim(ids_pad, begin, span, 0)
    query_ids = lax.dynamic_slice_in_dim(ids_all, begin, tokens, 0)
    key_rows = joined[:, :kv_cols].reshape(span, kv_heads, head_dim)
    value_rows = joined[:, kv_cols:].reshape(span, kv_heads, head_dim)
    block = math.gcd(tokens, 512)
    relative = (
        reach * tokens
        + jnp.arange(block, dtype=jnp.int32)[:, None]
        - jnp.arange(span, dtype=jnp.int32)[None, :]
    )
    allowed = (relative >= 0) & (relative < WINDOW) & (query_ids[0:block, None] == key_ids[None, :])
    scores = (
        jnp.einsum("tkgd,ukd->kgtu", queries, key_rows, preferred_element_type=jnp.float32)
        * attn_scale
    )
    scores = jnp.where(allowed[None, None], scores, -jnp.inf)
    top = jnp.max(scores, axis=-1, keepdims=True)
    expd = jnp.exp(scores - top)
    total = jnp.sum(expd, axis=-1, keepdims=True)
    probs = (expd / total).astype(jnp.bfloat16)
    mixed = jnp.einsum("kgtu,ukd->tkgd", probs, value_rows, preferred_element_type=jnp.float32)
    outputs = mixed.reshape(block, features).astype(jnp.bfloat16)
    n_fsdp = lax.axis_size("fsdp")
    n_seq = lax.axis_size("seq")
    each = out_weight.shape[0] // n_seq
    mine = lax.dynamic_slice_in_dim(out_weight, begin // tokens * each, each, 0)
    arranged = (
        outputs.reshape(tokens, n_fsdp, n_seq, each).transpose(0, 2, 1, 3).reshape(tokens, features)
    )
    partial_rows = lax.all_gather(mine, "fsdp", axis=0, tiled=True)
    all_rows = lax.all_gather(partial_rows, "seq", axis=0, tiled=True)
    projected = jnp.dot(arranged, all_rows, preferred_element_type=jnp.float32)
    meansq = jnp.mean(projected * projected, axis=-1, keepdims=True)
    result = (projected * lax.rsqrt(meansq + norm_eps) * post_gain).astype(jnp.bfloat16)
    return result[None]


def solution(mesh):
    in_specs = (
        P(("dp", "fsdp"), "seq", None),
        P(("dp", "fsdp"), "seq", None),
        P(("dp", "fsdp"), None),
        P(),
        P(),
        P("fsdp", None),
        P(),
    )
    out_specs = P(("dp", "fsdp"), "seq", None)
    return jax.shard_map(
        on_device, mesh=mesh, in_specs=in_specs, out_specs=out_specs, check_vma=False
    )
```

profile of v0, /device:TPU:64, one launch (start us, length us, event | category | flops | bytes accessed | tf_op | source)
XLA Modules:
  0.0 324.0 jit_solution(14192368447268685597)
XLA Ops:
  6.5 1.8 copy-done
  8.3 0.7 constant_dynamic-slice_fusion
  9.1 56.5 %all-gather.3.cloned.1.call-done = bf16[128,5376]{1,0:T(8,128)(2,1)} async-done(((bf16[16,5376]{1,0:T(8,128)(2,1)}), bf16[128,5376]{1,0:T(8,128)(2,1)}) %all-gather.3.cloned.1.call-update) | async-done | bytes 1376272 | tf_op jit(solution)/shard_map/all_gather | solution.py:98
  65.6 0.9 compare_reduce_fusion
  67.0 1.5 copy.26
  69.7 1.0 pad_maximum_fusion
  70.7 5.7 %collective-permute-start = (bf16[256,2048]{0,1:T(8,128)(2,1)}, bf16[256,2048]{0,1:T(8,128)(2,1)}, u32[]{:S(2)}, u32[]{:S(2)}) collective-permute-start(bf16[256,2048]{0,1:T(8,128)(2,1)} %pad_maximum_fusion), channel_id=1, source_target_pairs={{0,32},{8,40},{16,48},{24,56},{32,64},{40,72},{48,80},{56,88},{64,... | collective-permute-start | bytes 3145736 | tf_op jit(solution)/shard_map/ppermute | solution.py:15
  76.4 1.9 collective-permute-start.1
  78.3 2.6 collective-permute-start.2
  80.9 2.5 collective-permute-start.3
  84.2 0.6 multiply_reduce_fusion.1
  84.9 0.6 add_rsqrt_fusion
  85.5 0.8 copy.28
  86.4 1.4 multiply_multiply_fusion
  87.8 0.8 subtract_convert_fusion
  88.6 1.3 copy.31
  89.9 1.2 copy.32
  91.2 0.5 fusion.8
  91.7 48.3 %collective-permute-done = bf16[256,2048]{0,1:T(8,128)(2,1)} collective-permute-done((bf16[256,2048]{0,1:T(8,128)(2,1)}, bf16[256,2048]{0,1:T(8,128)(2,1)}, u32[]{:S(2)}, u32[]{:S(2)}) %collective-permute-start) | collective-permute-done | bytes 1048608 | tf_op jit(solution)/shard_map/ppermute | solution.py:15
  140.0 1.3 constant_dynamic-update-slice_fusion.4
  141.3 59.7 %collective-permute-done.1 = bf16[256,2048]{0,1:T(8,128)(2,1)} collective-permute-done((bf16[256,2048]{0,1:T(8,128)(2,1)}, bf16[256,2048]{0,1:T(8,128)(2,1)}, u32[]{:S(2)}, u32[]{:S(2)}) %collective-permute-start.1) | collective-permute-done | bytes 1048608 | tf_op jit(solution)/shard_map/ppermute | solution.py:15
  201.0 1.3 constant_dynamic-update-slice_fusion.3
  202.3 43.6 %collective-permute-done.2 = bf16[256,2048]{0,1:T(8,128)(2,1)} collective-permute-done((bf16[256,2048]{0,1:T(8,128)(2,1)}, bf16[256,2048]{0,1:T(8,128)(2,1)}, u32[]{:S(2)}, u32[]{:S(2)}) %collective-permute-start.2) | collective-permute-done | bytes 1048608 | tf_op jit(solution)/shard_map/ppermute | solution.py:15
  245.9 1.3 constant_dynamic-update-slice_fusion.2
  247.2 30.1 %collective-permute-done.3 = bf16[256,2048]{0,1:T(8,128)(2,1)} collective-permute-done((bf16[256,2048]{0,1:T(8,128)(2,1)}, bf16[256,2048]{0,1:T(8,128)(2,1)}, u32[]{:S(2)}, u32[]{:S(2)}) %collective-permute-start.3) | collective-permute-done | bytes 1048608 | tf_op jit(solution)/shard_map/ppermute | solution.py:15
  277.4 1.3 constant_dynamic-update-slice_fusion.1
  278.8 1.8 fusion.19
  280.6 8.7 %exponential_reduce_fusion = f32[8,2,256]{2,1,0:T(2,128)S(1)} fusion(bf16[1280,8,128,1]{0,2,3,1:T(8,128)(2,1)S(1)} %bitcast.63, pred[256,1280]{0,1:T(8,128)(4,1)S(1)} %fusion.8, bf16[256,8,2,64]{3,0,2,1:T(8,128)(2,1)} %bitcast.68, bf16[256,8,2,64]{3,0,2,1:T(8,128)(2,1)} %bitcast.66), kind=kOutput, calls=%fused_computation.4 | convolution fusion | flops 1365247232 | bytes 4014080 | tf_op jit(solution)/shard_map/sub | solution.py:86
  289.3 13.2 %fusion.4 = bf16[8,128,2,256]{3,1,2,0:T(8,128)(2,1)} fusion(bf16[1280,8,128,1]{0,2,3,1:T(8,128)(2,1)} %bitcast.65, f32[8,2,256]{2,1,0:T(2,128)S(1)} %exponential_reduce_fusion, bf16[1280,8,128,1]{0,2,3,1:T(8,128)(2,1)S(1)} %bitcast.64, pred[256,1280]{0,1:T(8,128)(4,1)S(1)} %fusion.8, bf16[256,8,2,64]{3,0,2,1:T(8,128)(2,1)} %bitcast.69, ...), kind=kOutput, calls=%fused_computation.14 | convolution fusion | flops 2713195776 | bytes 7684096 | tf_op jit(solution)/shard_map/kgtu,ukd->tkgd/dot_general | solution.py:89
  302.5 1.3 copy.35
  303.9 10.9 %multiply_reduce_fusion = (f32[256]{0:T(256)S(1)}, f32[256,5376]{1,0:T(8,128)S(1)}) fusion(bf16[256,2048]{0,1:T(8,128)(2,1)S(1)} %bitcast.62, bf16[2048,5376]{1,0:T(8,128)(2,1)} %all-gather.5.cloned.1.call-done), kind=kOutput, calls=%fused_computation.7 | convolution fusion | flops 5639897088 | bytes 28574720 | tf_op jit(solution)/shard_map/dot_general | solution.py:100
  314.9 2.1 fusion.3
  (41 shorter events, 2.9 us)
Async XLA Ops:
  6.5 1.8 copy-start
  6.5 59.1 %all-gather.3.cloned.1.call-start = ((), (), s32[]{:S(2)}) async-start(), calls=%async_computation | async-start | bytes 1548288 | tf_op jit(solution)/shard_map/all_gather | solution.py:98
  9.0 294.8 %all-gather.5.cloned.1.call-start = ((), (), s32[]{:S(2)}) async-start(), calls=%async_computation.1 | async-start | bytes 23396352 | tf_op jit(solution)/shard_map/all_gather | solution.py:99
  65.6 3.7 %copy-start.5 = (f32[128]{0:T(128)S(1)}, f32[128]{0:T(128)}, u32[]{:S(2)}) copy-start(f32[128]{0:T(128)} %param.11) | copy-start | bytes 1540
  69.5 14.1 %copy-start.2 = (bf16[1,256,2048]{2,1,0:T(8,128)(2,1)S(1)}, bf16[1,256,2048]{2,1,0:T(8,128)(2,1)}, u32[]{:S(2)}) copy-start(bf16[1,256,2048]{2,1,0:T(8,128)(2,1)} %param.7) | copy-start | bytes 3145732
  70.7 69.2 %collective-permute-start = (bf16[256,2048]{0,1:T(8,128)(2,1)}, bf16[256,2048]{0,1:T(8,128)(2,1)}, u32[]{:S(2)}, u32[]{:S(2)}) collective-permute-start(bf16[256,2048]{0,1:T(8,128)(2,1)} %pad_maximum_fusion), channel_id=1, source_target_pairs={{0,32},{8,40},{16,48},{24,56},{32,64},{40,72},{48,80},{56,88},{64,... | collective-permute-start | bytes 3145736 | tf_op jit(solution)/shard_map/ppermute | solution.py:15
  76.4 124.6 %collective-permute-start.1 = (bf16[256,2048]{0,1:T(8,128)(2,1)}, bf16[256,2048]{0,1:T(8,128)(2,1)}, u32[]{:S(2)}, u32[]{:S(2)}) collective-permute-start(bf16[256,2048]{0,1:T(8,128)(2,1)} %pad_maximum_fusion), channel_id=1, source_target_pairs={{0,24},{8,32},{16,40},{24,48},{32,56},{40,64},{48,72},{56,80},{64,... | collective-permute-start | bytes 3145736 | tf_op jit(solution)/shard_map/ppermute | solution.py:15
  78.3 167.6 %collective-permute-start.2 = (bf16[256,2048]{0,1:T(8,128)(2,1)}, bf16[256,2048]{0,1:T(8,128)(2,1)}, u32[]{:S(2)}, u32[]{:S(2)}) collective-permute-start(bf16[256,2048]{0,1:T(8,128)(2,1)} %pad_maximum_fusion), channel_id=1, source_target_pairs={{0,16},{8,24},{16,32},{24,40},{32,48},{40,56},{48,64},{56,72},{64,... | collective-permute-start | bytes 3145736 | tf_op jit(solution)/shard_map/ppermute | solution.py:15
  80.9 196.5 %collective-permute-start.3 = (bf16[256,2048]{0,1:T(8,128)(2,1)}, bf16[256,2048]{0,1:T(8,128)(2,1)}, u32[]{:S(2)}, u32[]{:S(2)}) collective-permute-start(bf16[256,2048]{0,1:T(8,128)(2,1)} %pad_maximum_fusion), channel_id=1, source_target_pairs={{0,8},{8,16},{16,24},{24,32},{32,40},{40,48},{48,56},{56,64},{64,7... | collective-permute-start | bytes 3145736 | tf_op jit(solution)/shard_map/ppermute | solution.py:15
  88.6 2.5 copy-start.3
  303.9 11.0 %copy-start.4 = (f32[5376]{0:T(1024)S(1)}, f32[5376]{0:T(1024)}, u32[]{:S(2)}) copy-start(f32[5376]{0:T(1024)} %param.13) | copy-start | bytes 64516
  314.8 2.3 copy-start.1
Sparse Core Ops, SparseCore 0:
  9.9 55.6 all-gather.2
  67.4 225.4 all-gather.4
where the time goes:
time: 325 us; the launch traced here: 324 us
  waiting for transfers between devices  238 us (73%)
  matrix products  32.8 us (10%)
  local copies, waits for them, and re-layouts  16.8 us (5%)
  between operations  13.7 us (4%)
  starting transfers between devices  12.7 us (4%)
  other arithmetic  9.65 us (3%)
    ppermute x4, waiting for transfers between devices, from_behind(): return lax.ppermute(block, axis, route)  182 us
    all_gather x1, waiting for transfers between devices, on_device(): partial_rows = lax.all_gather(mine, 'fsdp', axis=0, tiled=True)  56.5 us
    dot_general x1, matrix products, on_device(): jnp.einsum('kgtu,ukd->tkgd', probs, value_rows, preferred_element_type=jn...  13.2 us
    ppermute x4, starting transfers between devices, from_behind(): return lax.ppermute(block, axis, route)  12.6 us
    dot_general x1, matrix products, on_device(): projected = jnp.dot(arranged, all_rows, preferred_element_type=jnp.float32)  10.9 us
    unnamed x18, local copies, waits for them, and re-layouts  9.05 us
    sub x1, matrix products, on_device(): expd = jnp.exp(scores - top)  8.73 us
  transfers between devices with their start and end apart: 6, of which 5 were waited for; matrix products, arithmetic and copies ran while one was open for 13% of the time, Pallas kernels for 0%

commit v1 on v0

--- a/solution.py
+++ b/solution.py
@@ -96,7 +96,26 @@
         outputs.reshape(tokens, n_fsdp, n_seq, each).transpose(0, 2, 1, 3).reshape(tokens, features)
     )
     partial_rows = lax.all_gather(mine, "fsdp", axis=0, tiled=True)
-    all_rows = lax.all_gather(partial_rows, "seq", axis=0, tiled=True)
+    count_2, index_2, rows = (lax.axis_size("seq"), lax.axis_index("seq"), partial_rows.shape[0])
+    right = [(i_2, (i_2 + 1) % count_2) for i_2 in range(count_2)]
+    left = [(i_2, (i_2 - 1) % count_2) for i_2 in range(count_2)]
+    out = jnp.zeros(
+        (*partial_rows.shape[:0], count_2 * rows, *partial_rows.shape[0 + 1 :]), partial_rows.dtype
+    )
+    out = lax.dynamic_update_slice_in_dim(out, partial_rows, index_2 * rows, axis=0)
+    from_left = from_right = partial_rows
+    halfway = count_2 // 2
+    for step in range(1, halfway + 1):
+        from_left = lax.ppermute(from_left, "seq", right)
+        out = lax.dynamic_update_slice_in_dim(
+            out, from_left, (index_2 - step) % count_2 * rows, axis=0
+        )
+        if step < count_2 - halfway:
+            from_right = lax.ppermute(from_right, "seq", left)
+            out = lax.dynamic_update_slice_in_dim(
+                out, from_right, (index_2 + step) % count_2 * rows, axis=0
+            )
+    all_rows = out
     projected = jnp.dot(arranged, all_rows, preferred_element_type=jnp.float32)
     meansq = jnp.mean(projected * projected, axis=-1, keepdims=True)
     result = (projected * lax.rsqrt(meansq + norm_eps) * post_gain).astype(jnp.bfloat16)

time: 325 us -> 328 us (level)
  the two profiles are of different devices: /device:TPU:64 before, /device:TPU:140 now
where the time goes in v1:
time: 328 us; the launch traced here: 327 us
  waiting for transfers between devices  191 us (58%)
  local copies, waits for them, and re-layouts  46.1 us (14%)
  matrix products  32.9 us (10%)
  starting transfers between devices  30.8 us (9%)
  between operations  14 us (4%)
  other arithmetic  12.5 us (4%)
    ppermute x8, waiting for transfers between devices, on_device(): from_left = lax.ppermute(from_left, 'seq', right)  95.7 us
    ppermute x4, waiting for transfers between devices, from_behind(): return lax.ppermute(block, axis, route)  95.2 us
    ppermute x7, starting transfers between devices, on_device(): from_right = lax.ppermute(from_right, 'seq', left)  20.7 us
    dot_general x1, matrix products, on_device(): jnp.einsum('kgtu,ukd->tkgd', probs, value_rows, preferred_element_type=jn...  13.2 us
    dot_general x1, matrix products, on_device(): projected = jnp.dot(arranged, all_rows, preferred_element_type=jnp.float32)  11 us
    dynamic_update_slice x8, local copies, waits for them, and re-layouts, on_device(): lax.dynamic_update_slice_in_dim(out, from_left, (index_2 - step) % count_...  10.9 us
    ppermute x4, starting transfers between devices, from_behind(): return lax.ppermute(block, axis, route)  10.1 us
    dynamic_update_slice x7, local copies, waits for them, and re-layouts, on_device(): lax.dynamic_update_slice_in_dim(out, from_right, (index_2 + step) % count...  9.7 us
  transfers between devices with their start and end apart: 20, of which 11 were waited for; matrix products, arithmetic and copies ran while one was open for 21% of the time, Pallas kernels for 0%

profile of v1, /device:TPU:140, one launch (start us, length us, event | category | flops | bytes accessed | tf_op | source)
XLA Modules:
  0.0 327.2 jit_solution(16188892963323051119)
XLA Ops:
  6.6 2.4 copy.26
  16.5 3.4 %collective-permute-start = (bf16[256,2048]{0,1:T(8,128)(2,1)}, bf16[256,2048]{0,1:T(8,128)(2,1)}, u32[]{:S(2)}, u32[]{:S(2)}) collective-permute-start(bf16[256,2048]{0,1:T(8,128)(2,1)} %pad_maximum_fusion), channel_id=1, source_target_pairs={{0,32},{8,40},{16,48},{24,56},{32,64},{40,72},{48,80},{56,88},{64,... | collective-permute-start | bytes 3145736 | tf_op jit(solution)/shard_map/ppermute | solution.py:15
  19.9 2.1 collective-permute-start.1
  22.0 2.8 collective-permute-start.2
  24.8 1.9 collective-permute-start.3
  27.9 1.5 convert_bitcast_fusion
  36.1 12.8 %collective-permute-done = bf16[256,2048]{0,1:T(8,128)(2,1)} collective-permute-done((bf16[256,2048]{0,1:T(8,128)(2,1)}, bf16[256,2048]{0,1:T(8,128)(2,1)}, u32[]{:S(2)}, u32[]{:S(2)}) %collective-permute-start) | collective-permute-done | bytes 1048608 | tf_op jit(solution)/shard_map/ppermute | solution.py:15
  50.1 50.6 %collective-permute-done.1 = bf16[256,2048]{0,1:T(8,128)(2,1)} collective-permute-done((bf16[256,2048]{0,1:T(8,128)(2,1)}, bf16[256,2048]{0,1:T(8,128)(2,1)}, u32[]{:S(2)}, u32[]{:S(2)}) %collective-permute-start.1) | collective-permute-done | bytes 1048608 | tf_op jit(solution)/shard_map/ppermute | solution.py:15
  102.0 22.5 %collective-permute-done.2 = bf16[256,2048]{0,1:T(8,128)(2,1)} collective-permute-done((bf16[256,2048]{0,1:T(8,128)(2,1)}, bf16[256,2048]{0,1:T(8,128)(2,1)}, u32[]{:S(2)}, u32[]{:S(2)}) %collective-permute-start.2) | collective-permute-done | bytes 1048608 | tf_op jit(solution)/shard_map/ppermute | solution.py:15
  125.8 9.4 %collective-permute-done.3 = bf16[256,2048]{0,1:T(8,128)(2,1)} collective-permute-done((bf16[256,2048]{0,1:T(8,128)(2,1)}, bf16[256,2048]{0,1:T(8,128)(2,1)}, u32[]{:S(2)}, u32[]{:S(2)}) %collective-permute-start.3) | collective-permute-done | bytes 1048608 | tf_op jit(solution)/shard_map/ppermute | solution.py:15
  136.6 1.8 fusion.19
  138.4 3.0 collective-permute-start.5
  141.3 8.7 %exponential_reduce_fusion = f32[8,2,256]{2,1,0:T(2,128)S(1)} fusion(bf16[1280,8,128,1]{0,2,3,1:T(8,128)(2,1)S(1)} %bitcast.63, pred[256,1280]{0,1:T(8,128)(4,1)S(1)} %copy-done.5, bf16[256,8,2,64]{3,0,2,1:T(8,128)(2,1)} %bitcast.68, bf16[256,8,2,64]{3,0,2,1:T(8,128)(2,1)} %bitcast.66), kind=kOutput, calls=%fused_computation.4 | convolution fusion | flops 1365247232 | bytes 4014080 | tf_op jit(solution)/shard_map/sub | solution.py:86
  150.1 13.2 %fusion.4 = bf16[8,128,2,256]{3,1,2,0:T(8,128)(2,1)} fusion(bf16[1280,8,128,1]{0,2,3,1:T(8,128)(2,1)} %bitcast.65, f32[8,2,256]{2,1,0:T(2,128)S(1)} %exponential_reduce_fusion, bf16[1280,8,128,1]{0,2,3,1:T(8,128)(2,1)S(1)} %bitcast.64, pred[256,1280]{0,1:T(8,128)(4,1)S(1)} %copy-done.5, bf16[256,8,2,64]{3,0,2,1:T(8,128)(2,1)} %bitcast.69, ...), kind=kOutput, calls=%fused_computation.14 | convolution fusion | flops 2713195776 | bytes 7684096 | tf_op jit(solution)/shard_map/kgtu,ukd->tkgd/dot_general | solution.py:89
  164.6 7.5 %broadcast_in_dim.19 = bf16[2048,5376]{1,0:T(8,128)(2,1)} broadcast(bf16[]{:T(256)} %constant.147.clone.1), dimensions={} | broadcast | bytes 22020098 | tf_op jit(solution)/shard_map/broadcast_in_dim | solution.py:102
  173.2 3.0 collective-permute-start.7
  176.2 2.5 constant_dynamic-update-slice_fusion.19
  178.7 2.6 constant_dynamic-update-slice_fusion.18
  181.3 11.1 %collective-permute-done.6 = bf16[128,5376]{1,0:T(8,128)(2,1)S(1)} collective-permute-done((bf16[128,5376]{1,0:T(8,128)(2,1)}, bf16[128,5376]{1,0:T(8,128)(2,1)S(1)}, u32[]{:S(2)}, u32[]{:S(2)}) %collective-permute-start.6) | collective-permute-done | bytes 1376288 | tf_op jit(solution)/shard_map/ppermute | solution.py:109
  192.4 3.0 collective-permute-start.9
  197.8 13.6 %collective-permute-done.8 = bf16[128,5376]{1,0:T(8,128)(2,1)S(1)} collective-permute-done((bf16[128,5376]{1,0:T(8,128)(2,1)S(1)}, bf16[128,5376]{1,0:T(8,128)(2,1)S(1)}, u32[]{:S(2)}, u32[]{:S(2)}) %collective-permute-start.8) | collective-permute-done | bytes 1376288 | tf_op jit(solution)/shard_map/ppermute | solution.py:109
  211.3 3.0 collective-permute-start.11
  216.6 13.6 %collective-permute-done.10 = bf16[128,5376]{1,0:T(8,128)(2,1)S(1)} collective-permute-done((bf16[128,5376]{1,0:T(8,128)(2,1)S(1)}, bf16[128,5376]{1,0:T(8,128)(2,1)S(1)}, u32[]{:S(2)}, u32[]{:S(2)}) %collective-permute-start.10) | collective-permute-done | bytes 1376288 | tf_op jit(solution)/shard_map/ppermute | solution.py:109
  230.3 3.0 collective-permute-start.13
  235.6 13.6 %collective-permute-done.12 = bf16[128,5376]{1,0:T(8,128)(2,1)S(1)} collective-permute-done((bf16[128,5376]{1,0:T(8,128)(2,1)S(1)}, bf16[128,5376]{1,0:T(8,128)(2,1)S(1)}, u32[]{:S(2)}, u32[]{:S(2)}) %collective-permute-start.12) | collective-permute-done | bytes 1376288 | tf_op jit(solution)/shard_map/ppermute | solution.py:109
  249.2 3.0 collective-permute-start.15
  254.6 13.6 %collective-permute-done.14 = bf16[128,5376]{1,0:T(8,128)(2,1)S(1)} collective-permute-done((bf16[128,5376]{1,0:T(8,128)(2,1)S(1)}, bf16[128,5376]{1,0:T(8,128)(2,1)S(1)}, u32[]{:S(2)}, u32[]{:S(2)}) %collective-permute-start.14) | collective-permute-done | bytes 1376288 | tf_op jit(solution)/shard_map/ppermute | solution.py:109
  268.2 3.0 collective-permute-start.17
  273.5 13.6 %collective-permute-done.16 = bf16[128,5376]{1,0:T(8,128)(2,1)S(1)} collective-permute-done((bf16[128,5376]{1,0:T(8,128)(2,1)S(1)}, bf16[128,5376]{1,0:T(8,128)(2,1)S(1)}, u32[]{:S(2)}, u32[]{:S(2)}) %collective-permute-start.16) | collective-permute-done | bytes 1376288 | tf_op jit(solution)/shard_map/ppermute | solution.py:109
  289.4 16.6 %collective-permute-done.18 = bf16[128,5376]{1,0:T(8,128)(2,1)S(1)} collective-permute-done((bf16[128,5376]{1,0:T(8,128)(2,1)S(1)}, bf16[128,5376]{1,0:T(8,128)(2,1)S(1)}, u32[]{:S(2)}, u32[]{:S(2)}) %collective-permute-start.18) | collective-permute-done | bytes 1376288 | tf_op jit(solution)/shard_map/ppermute | solution.py:109
  307.3 11.0 %multiply_reduce_fusion = (f32[256]{0:T(256)S(1)}, f32[256,5376]{1,0:T(8,128)S(1)}) fusion(bf16[256,2048]{0,1:T(8,128)(2,1)S(1)} %bitcast.62, bf16[2048,5376]{1,0:T(8,128)(2,1)} %constant_dynamic-update-slice_fusion.5), kind=kOutput, calls=%fused_computation.7 | convolution fusion | flops 5639897088 | bytes 28574720 | tf_op jit(solution)/shard_map/dot_general | solution.py:119
  318.2 2.1 fusion.3
  (91 shorter events, 38.2 us)
Async XLA Ops:
  6.5 20.2 %copy-start = (bf16[256,5376]{1,0:T(8,128)(2,1)S(1)}, bf16[256,5376]{1,0:T(8,128)(2,1)}, u32[]{:S(2)}) copy-start(bf16[256,5376]{1,0:T(8,128)(2,1)} %param.12) | copy-start | bytes 8257540
  6.5 131.8 %all-gather.2.cloned.1.call-start = ((), (), s32[]{:S(2)}) async-start(), calls=%async_computation | async-start | bytes 1548288 | tf_op jit(solution)/shard_map/all_gather | solution.py:98
  14.7 0.8 copy-start.2
  16.5 32.3 %collective-permute-start = (bf16[256,2048]{0,1:T(8,128)(2,1)}, bf16[256,2048]{0,1:T(8,128)(2,1)}, u32[]{:S(2)}, u32[]{:S(2)}) collective-permute-start(bf16[256,2048]{0,1:T(8,128)(2,1)} %pad_maximum_fusion), channel_id=1, source_target_pairs={{0,32},{8,40},{16,48},{24,56},{32,64},{40,72},{48,80},{56,88},{64,... | collective-permute-start | bytes 3145736 | tf_op jit(solution)/shard_map/ppermute | solution.py:15
  19.9 80.8 %collective-permute-start.1 = (bf16[256,2048]{0,1:T(8,128)(2,1)}, bf16[256,2048]{0,1:T(8,128)(2,1)}, u32[]{:S(2)}, u32[]{:S(2)}) collective-permute-start(bf16[256,2048]{0,1:T(8,128)(2,1)} %pad_maximum_fusion), channel_id=1, source_target_pairs={{0,24},{8,32},{16,40},{24,48},{32,56},{40,64},{48,72},{56,80},{64,... | collective-permute-start | bytes 3145736 | tf_op jit(solution)/shard_map/ppermute | solution.py:15
  22.0 102.5 %collective-permute-start.2 = (bf16[256,2048]{0,1:T(8,128)(2,1)}, bf16[256,2048]{0,1:T(8,128)(2,1)}, u32[]{:S(2)}, u32[]{:S(2)}) collective-permute-start(bf16[256,2048]{0,1:T(8,128)(2,1)} %pad_maximum_fusion), channel_id=1, source_target_pairs={{0,16},{8,24},{16,32},{24,40},{32,48},{40,56},{48,64},{56,72},{64,... | collective-permute-start | bytes 3145736 | tf_op jit(solution)/shard_map/ppermute | solution.py:15
  24.8 110.4 %collective-permute-start.3 = (bf16[256,2048]{0,1:T(8,128)(2,1)}, bf16[256,2048]{0,1:T(8,128)(2,1)}, u32[]{:S(2)}, u32[]{:S(2)}) collective-permute-start(bf16[256,2048]{0,1:T(8,128)(2,1)} %pad_maximum_fusion), channel_id=1, source_target_pairs={{0,8},{8,16},{16,24},{24,32},{32,40},{40,48},{48,56},{56,64},{64,7... | collective-permute-start | bytes 3145736 | tf_op jit(solution)/shard_map/ppermute | solution.py:15
  27.6 3.0 copy-start.8
  31.4 3.3 %copy-start.6 = (s32[1,4096]{1,0:T(1,128)S(1)}, s32[1,4096]{1,0:T(1,128)}, u32[]{:S(2)}) copy-start(s32[1,4096]{1,0:T(1,128)} %param.9) | copy-start | bytes 49156
  33.5 102.9 %copy-start.3 = (bf16[256,8,128]{0,2,1:T(8,128)(2,1)S(1)}, bf16[256,8,128]{0,2,1:T(8,128)(2,1)}, u32[]{:S(2)}) copy-start(bf16[256,8,128]{0,2,1:T(8,128)(2,1)} %copy-done.2) | copy-start | bytes 1572868
  136.5 4.8 %copy-start.5 = (pred[256,1280]{0,1:T(8,128)(4,1)S(1)}, pred[256,1280]{0,1:T(8,128)(4,1)}, u32[]{:S(2)}) copy-start(pred[256,1280]{0,1:T(8,128)(4,1)} %fusion.8) | copy-start | bytes 983044
  138.4 34.8 %collective-permute-start.4 = (bf16[128,5376]{1,0:T(8,128)(2,1)}, bf16[128,5376]{1,0:T(8,128)(2,1)}, u32[]{:S(2)}, u32[]{:S(2)}) collective-permute-start(bf16[128,5376]{1,0:T(8,128)(2,1)} %all-gather.2.cloned.1.call-done), channel_id=1, source_target_pairs={{0,8},{8,16},{16,24},{24,32},{32,40},{40,48},{48,56},{56,64},{64,7... | collective-permute-start | bytes 4128776 | tf_op jit(solution)/shard_map/ppermute | solution.py:109
  138.4 34.8 %collective-permute-start.5 = (bf16[128,5376]{1,0:T(8,128)(2,1)}, bf16[128,5376]{1,0:T(8,128)(2,1)}, u32[]{:S(2)}, u32[]{:S(2)}) collective-permute-start(bf16[128,5376]{1,0:T(8,128)(2,1)} %all-gather.2.cloned.1.call-done), channel_id=1, source_target_pairs={{0,120},{8,0},{16,8},{24,16},{32,24},{40,32},{48,40},{56,48},{64,5... | collective-permute-start | bytes 4128776 | tf_op jit(solution)/shard_map/ppermute | solution.py:114
  164.6 7.5 %copy-start.4 = (bf16[128,5376]{1,0:T(8,128)(2,1)S(1)}, bf16[128,5376]{1,0:T(8,128)(2,1)}, u32[]{:S(2)}) copy-start(bf16[128,5376]{1,0:T(8,128)(2,1)} %all-gather.2.cloned.1.call-done) | copy-start | bytes 4128772
  173.2 19.2 %collective-permute-start.6 = (bf16[128,5376]{1,0:T(8,128)(2,1)}, bf16[128,5376]{1,0:T(8,128)(2,1)S(1)}, u32[]{:S(2)}, u32[]{:S(2)}) collective-permute-start(bf16[128,5376]{1,0:T(8,128)(2,1)} %collective-permute-done.4), channel_id=1, source_target_pairs={{0,8},{8,16},{16,24},{24,32},{32,40},{40,48},{48,56},{56,64},{64,7... | collective-permute-start | bytes 4128776 | tf_op jit(solution)/shard_map/ppermute | solution.py:109
  173.2 19.2 %collective-permute-start.7 = (bf16[128,5376]{1,0:T(8,128)(2,1)}, bf16[128,5376]{1,0:T(8,128)(2,1)S(1)}, u32[]{:S(2)}, u32[]{:S(2)}) collective-permute-start(bf16[128,5376]{1,0:T(8,128)(2,1)} %collective-permute-done.5), channel_id=1, source_target_pairs={{0,120},{8,0},{16,8},{24,16},{32,24},{40,32},{48,40},{56,48},{64,5... | collective-permute-start | bytes 4128776 | tf_op jit(solution)/shard_map/ppermute | solution.py:114
  192.4 18.9 %collective-permute-start.8 = (bf16[128,5376]{1,0:T(8,128)(2,1)S(1)}, bf16[128,5376]{1,0:T(8,128)(2,1)S(1)}, u32[]{:S(2)}, u32[]{:S(2)}) collective-permute-start(bf16[128,5376]{1,0:T(8,128)(2,1)S(1)} %collective-permute-done.6), channel_id=1, source_target_pairs={{0,8},{8,16},{16,24},{24,32},{32,40},{40,48},{48,56},{56,64},{64,7... | collective-permute-start | bytes 4128776 | tf_op jit(solution)/shard_map/ppermute | solution.py:109
  192.4 18.9 %collective-permute-start.9 = (bf16[128,5376]{1,0:T(8,128)(2,1)S(1)}, bf16[128,5376]{1,0:T(8,128)(2,1)S(1)}, u32[]{:S(2)}, u32[]{:S(2)}) collective-permute-start(bf16[128,5376]{1,0:T(8,128)(2,1)S(1)} %collective-permute-done.7), channel_id=1, source_target_pairs={{0,120},{8,0},{16,8},{24,16},{32,24},{40,32},{48,40},{56,48},{64,5... | collective-permute-start | bytes 4128776 | tf_op jit(solution)/shard_map/ppermute | solution.py:114
  211.3 18.9 %collective-permute-start.10 = (bf16[128,5376]{1,0:T(8,128)(2,1)S(1)}, bf16[128,5376]{1,0:T(8,128)(2,1)S(1)}, u32[]{:S(2)}, u32[]{:S(2)}) collective-permute-start(bf16[128,5376]{1,0:T(8,128)(2,1)S(1)} %collective-permute-done.8), channel_id=1, source_target_pairs={{0,8},{8,16},{16,24},{24,32},{32,40},{40,48},{48,56},{56,64},{64,7... | collective-permute-start | bytes 4128776 | tf_op jit(solution)/shard_map/ppermute | solution.py:109
  211.3 18.9 %collective-permute-start.11 = (bf16[128,5376]{1,0:T(8,128)(2,1)S(1)}, bf16[128,5376]{1,0:T(8,128)(2,1)S(1)}, u32[]{:S(2)}, u32[]{:S(2)}) collective-permute-start(bf16[128,5376]{1,0:T(8,128)(2,1)S(1)} %collective-permute-done.9), channel_id=1, source_target_pairs={{0,120},{8,0},{16,8},{24,16},{32,24},{40,32},{48,40},{56,48},{64,5... | collective-permute-start | bytes 4128776 | tf_op jit(solution)/shard_map/ppermute | solution.py:114
  230.3 18.9 %collective-permute-start.12 = (bf16[128,5376]{1,0:T(8,128)(2,1)S(1)}, bf16[128,5376]{1,0:T(8,128)(2,1)S(1)}, u32[]{:S(2)}, u32[]{:S(2)}) collective-permute-start(bf16[128,5376]{1,0:T(8,128)(2,1)S(1)} %collective-permute-done.10), channel_id=1, source_target_pairs={{0,8},{8,16},{16,24},{24,32},{32,40},{40,48},{48,56},{56,64},{64,7... | collective-permute-start | bytes 4128776 | tf_op jit(solution)/shard_map/ppermute | solution.py:109
  230.3 18.9 %collective-permute-start.13 = (bf16[128,5376]{1,0:T(8,128)(2,1)S(1)}, bf16[128,5376]{1,0:T(8,128)(2,1)S(1)}, u32[]{:S(2)}, u32[]{:S(2)}) collective-permute-start(bf16[128,5376]{1,0:T(8,128)(2,1)S(1)} %collective-permute-done.11), channel_id=1, source_target_pairs={{0,120},{8,0},{16,8},{24,16},{32,24},{40,32},{48,40},{56,48},{64,5... | collective-permute-start | bytes 4128776 | tf_op jit(solution)/shard_map/ppermute | solution.py:114
  249.2 18.9 %collective-permute-start.14 = (bf16[128,5376]{1,0:T(8,128)(2,1)S(1)}, bf16[128,5376]{1,0:T(8,128)(2,1)S(1)}, u32[]{:S(2)}, u32[]{:S(2)}) collective-permute-start(bf16[128,5376]{1,0:T(8,128)(2,1)S(1)} %collective-permute-done.12), channel_id=1, source_target_pairs={{0,8},{8,16},{16,24},{24,32},{32,40},{40,48},{48,56},{56,64},{64,7... | collective-permute-start | bytes 4128776 | tf_op jit(solution)/shard_map/ppermute | solution.py:109
  249.2 18.9 %collective-permute-start.15 = (bf16[128,5376]{1,0:T(8,128)(2,1)S(1)}, bf16[128,5376]{1,0:T(8,128)(2,1)S(1)}, u32[]{:S(2)}, u32[]{:S(2)}) collective-permute-start(bf16[128,5376]{1,0:T(8,128)(2,1)S(1)} %collective-permute-done.13), channel_id=1, source_target_pairs={{0,120},{8,0},{16,8},{24,16},{32,24},{40,32},{48,40},{56,48},{64,5... | collective-permute-start | bytes 4128776 | tf_op jit(solution)/shard_map/ppermute | solution.py:114
  268.2 18.9 %collective-permute-start.16 = (bf16[128,5376]{1,0:T(8,128)(2,1)S(1)}, bf16[128,5376]{1,0:T(8,128)(2,1)S(1)}, u32[]{:S(2)}, u32[]{:S(2)}) collective-permute-start(bf16[128,5376]{1,0:T(8,128)(2,1)S(1)} %collective-permute-done.14), channel_id=1, source_target_pairs={{0,8},{8,16},{16,24},{24,32},{32,40},{40,48},{48,56},{56,64},{64,7... | collective-permute-start | bytes 4128776 | tf_op jit(solution)/shard_map/ppermute | solution.py:109
  268.2 20.1 %collective-permute-start.17 = (bf16[128,5376]{1,0:T(8,128)(2,1)S(1)}, bf16[128,5376]{1,0:T(8,128)(2,1)S(1)}, u32[]{:S(2)}, u32[]{:S(2)}) collective-permute-start(bf16[128,5376]{1,0:T(8,128)(2,1)S(1)} %collective-permute-done.15), channel_id=1, source_target_pairs={{0,120},{8,0},{16,8},{24,16},{32,24},{40,32},{48,40},{56,48},{64,5... | collective-permute-start | bytes 4128776 | tf_op jit(solution)/shard_map/ppermute | solution.py:114
  287.1 18.9 %collective-permute-start.18 = (bf16[128,5376]{1,0:T(8,128)(2,1)S(1)}, bf16[128,5376]{1,0:T(8,128)(2,1)S(1)}, u32[]{:S(2)}, u32[]{:S(2)}) collective-permute-start(bf16[128,5376]{1,0:T(8,128)(2,1)S(1)} %collective-permute-done.16), channel_id=1, source_target_pairs={{0,8},{8,16},{16,24},{24,32},{32,40},{40,48},{48,56},{56,64},{64,7... | collective-permute-start | bytes 4128776 | tf_op jit(solution)/shard_map/ppermute | solution.py:109
  307.3 11.0 %copy-start.7 = (f32[5376]{0:T(1024)S(1)}, f32[5376]{0:T(1024)}, u32[]{:S(2)}) copy-start(f32[5376]{0:T(1024)} %param.13) | copy-start | bytes 64516
  307.3 13.1 %copy-start.1 = (bf16[256,5376]{1,0:T(8,128)(2,1)S(1)}, bf16[256,5376]{1,0:T(8,128)(2,1)}, u32[]{:S(2)}) copy-start(bf16[256,5376]{1,0:T(8,128)(2,1)} %param.12) | copy-start | bytes 8257540
Sparse Core Ops, SparseCore 0:
  27.5 53.5 all-gather.1
